TPU v7x, 256 devices: a whole 4x4x8 slice. The times are simulated.
256 devices in a mesh: src: 16 (over x, y_lo, core), rcv: 16 (over y_hi, z).
Axes of the slice: x: 4, y: 4 (y_hi: 2, y_lo: 2; y = y_hi * 2 + y_lo), z: 8, core: 2. Of those that a mesh axis runs over, the one named last changes fastest.
Arguments:
- data: bfloat16 [2, 512, 512, 256], P(None, 'src', 'rcv'), as said below
- panel_index: int32 [2, 32], replicated, may hold values from 0 to 511, as said below
- panel_weight: float32 [2, 32], replicated, may hold values from 0.25 to 1.75
- band_index: int32 [256], replicated, may hold values from 1 to 512, as said below
Outputs:
- predicted: bfloat16 [512, 512, 1024], P('src', 'rcv')
Inputs may be any that keep to these rules, and one draw needn't show every extreme that they name: data is unchanged when the source and receiver indices are exchanged (reciprocity). `panel_index`: each row holds the 32 traces of one aligned group of 32 trace numbers, each once, in some order; one row holds the first group and another the last. `band_index`: distinct bins.
All inputs are finite; a program needn't handle non-finite values.
Results may differ from a plain program's by a relative error of at most 0.0062.
Values may be sent and summed in bfloat16 or wider, within the bound.
A program may use at most 128 MiB of HBM per device.

v0:
```python
import math

import jax
import jax.numpy as jnp
from jax import lax
from jax.sharding import PartitionSpec as P

NF = 256
NT = 1024
PANEL = 32
STEPS = 2


def spread(block, axis, holder):
    block = jnp.where(lax.axis_index(axis) == holder, block, jnp.zeros_like(block))
    return lax.psum(block, axis)


def phase_table(band_index):
    sample_times = jnp.arange(NT, dtype=jnp.int32)
    phase_turns = band_index[:, None] * sample_times[None, :] % NT
    phase_angle = phase_turns.astype(jnp.float32) * (2.0 * math.pi / NT)
    cos_table = jnp.cos(phase_angle).astype(jnp.bfloat16)
    sin_table = jnp.sin(phase_angle).astype(jnp.bfloat16)
    return jnp.concatenate([cos_table, -sin_table], axis=0)


def body(data, panel_index, panel_weight, band_index):
    src_rows = data.shape[1]
    rcv_cols = data.shape[2]
    freq_count = data.shape[3]
    here_src = lax.axis_index("src")
    here_rcv = lax.axis_index("rcv")
    wave_table = phase_table(band_index)
    norm_scale = 1.0 / math.sqrt(2.0 * STEPS * PANEL * NF)
    spec_re = jnp.zeros((src_rows, rcv_cols, freq_count), jnp.float32)
    spec_im = jnp.zeros((src_rows, rcv_cols, freq_count), jnp.float32)
    for step_index in range(panel_index.shape[0]):
        traces = panel_index[step_index]
        owner_rcv = traces[0] // rcv_cols
        owner_src = traces[0] // src_rows
        local_cols = jnp.clip(traces - here_rcv * rcv_cols, 0, rcv_cols - 1)
        picked = jnp.take(data, local_cols, axis=2)
        columns = spread(picked, "rcv", owner_rcv)
        local_rows = jnp.clip(traces - here_src * src_rows, 0, src_rows - 1)
        right_panel = spread(jnp.take(data, local_rows, axis=1), "src", owner_src)
        product_form = "spf,prf->srf"
        weighted = (
            columns.astype(jnp.float32) * panel_weight[step_index][None, None, :, None]
        ).astype(jnp.bfloat16)
        spec_re = spec_re + jnp.einsum(
            product_form, weighted[0], right_panel[0], preferred_element_type=jnp.float32
        )
        spec_re = spec_re - jnp.einsum(
            product_form, weighted[1], right_panel[1], preferred_element_type=jnp.float32
        )
        spec_im = spec_im + jnp.einsum(
            product_form, weighted[0], right_panel[1], preferred_element_type=jnp.float32
        )
        spec_im = spec_im + jnp.einsum(
            product_form, weighted[1], right_panel[0], preferred_element_type=jnp.float32
        )
    stacked = (
        jnp.concatenate([spec_re, spec_im], axis=2)
        .reshape(src_rows * rcv_cols, 2 * freq_count)
        .astype(jnp.bfloat16)
    )
    traces_time = jnp.dot(stacked, wave_table, preferred_element_type=jnp.float32)
    return (-norm_scale * traces_time).reshape(src_rows, rcv_cols, NT).astype(jnp.bfloat16)


def solution(mesh):
    placed = (P(None, "src", "rcv", None), P(), P(), P())
    return jax.shard_map(
        body, mesh=mesh, in_specs=placed, out_specs=P("src", "rcv", None), check_vma=False
    )
```

profile of v0, /device:TPU:5, one launch (start us, length us, event | category | flops | bytes accessed | tf_op | source)
XLA Modules:
  0.0 496.0 jit_solution(14026082580485608483)
XLA Ops:
  6.5 1.4 fusion.19
  14.1 3.6 gather_fusion.1
  17.7 6.5 %copy.27 = bf16[32,2,32,256]{0,2,3,1:T(8,128)(2,1)} copy(bf16[32,2,32,256]{3,0,2,1:T(8,128)(2,1)S(1)} %gather_fusion.1) | data formatting | bytes 2097152 | tf_op jit(solution)/shard_map/jit(_take)/gather | solution.py:43
  24.1 3.6 gather_fusion.3
  27.7 6.5 %copy.31 = bf16[32,2,32,256]{0,2,3,1:T(8,128)(2,1)} copy(bf16[32,2,32,256]{3,0,2,1:T(8,128)(2,1)S(1)} %gather_fusion.3) | data formatting | bytes 2097152 | tf_op jit(solution)/shard_map/jit(_take)/gather | solution.py:43
  34.2 6.0 %bitcast_select_fusion = (bf16[2,32,32,256]{2,1,3,0:T(8,128)(2,1)}, bf16[2,32,32,256]{2,1,3,0:T(8,128)(2,1)}) fusion(bf16[32,2,32,256]{0,2,3,1:T(8,128)(2,1)} %copy.31, pred[32]{0:T(512)(128)(4,1)S(1)} %get-tuple-element.23, pred[]{:T(512)S(6)} %eq.17, bf16[32,2,32,256]{0,2,3,1:T(8,128)(2,1)} %copy.27, pred[32]{0:T(512)(128)(4,1)S(1)} %get-tuple-element.21, ...), kind=kLoop, calls=%fused_computation.6 | loop fusion | flops 2097152 | bytes 4194370 | tf_op jit(solution)/shard_map/jit(_where)/select_n | solution.py:15
  41.0 6.5 %copy.26 = bf16[32,2,32,256]{2,0,3,1:T(8,128)(2,1)} copy(bf16[32,2,32,256]{3,2,1,0:T(8,128)(2,1)S(1)} %gather_fusion) | data formatting | bytes 2097152 | tf_op jit(solution)/shard_map/jit(_take)/gather | solution.py:46
  48.2 6.5 %copy.30 = bf16[32,2,32,256]{2,0,3,1:T(8,128)(2,1)} copy(bf16[32,2,32,256]{3,2,1,0:T(8,128)(2,1)S(1)} %gather_fusion.2) | data formatting | bytes 2097152 | tf_op jit(solution)/shard_map/jit(_take)/gather | solution.py:46
  54.7 6.2 %bitcast_select_fusion.1 = (bf16[2,32,32,256]{2,1,3,0:T(8,128)(2,1)}, bf16[2,32,32,256]{2,1,3,0:T(8,128)(2,1)}) fusion(bf16[32,2,32,256]{2,0,3,1:T(8,128)(2,1)} %copy.30, pred[32]{0:T(512)(128)(4,1)S(1)} %get-tuple-element.25, pred[]{:T(512)S(6)} %eq.16, bf16[32,2,32,256]{2,0,3,1:T(8,128)(2,1)} %copy.26, pred[32]{0:T(512)(128)(4,1)S(1)} %get-tuple-element.11, ...), kind=kLoop, calls=%fused_computation.7 | loop fusion | flops 2097152 | bytes 4194370 | tf_op jit(solution)/shard_map/jit(_where)/select_n | solution.py:15
  61.5 4.8 cosine_convert_fusion
  66.3 4.9 fusion.17
  71.2 177.9 %all-reduce.5.cloned.1.call-done = (bf16[2,32,32,256]{2,1,3,0:T(8,128)(2,1)}, bf16[2,32,32,256]{2,1,3,0:T(8,128)(2,1)}) async-done(((bf16[2,32,32,256]{2,1,3,0:T(8,128)(2,1)}, bf16[2,32,32,256]{2,1,3,0:T(8,128)(2,1)}), (bf16[2,32,32,256]{2,1,3,0:T(8,128)(2,1)}, bf16[2,32,32,256]{2,1,3,0:T(8,128)(2,1)})) %all-reduce.5.cloned.1.call-update) | async-done | bytes 2097168 | tf_op jit(solution)/shard_map/psum | solution.py:16
  249.1 5.0 multiply_convert_fusion.1
  254.0 195.5 %all-reduce.7.cloned.1.call-done = (bf16[2,32,32,256]{2,1,3,0:T(8,128)(2,1)}, bf16[2,32,32,256]{2,1,3,0:T(8,128)(2,1)}) async-done(((bf16[2,32,32,256]{2,1,3,0:T(8,128)(2,1)}, bf16[2,32,32,256]{2,1,3,0:T(8,128)(2,1)}), (bf16[2,32,32,256]{2,1,3,0:T(8,128)(2,1)}, bf16[2,32,32,256]{2,1,3,0:T(8,128)(2,1)})) %all-reduce.7.cloned.1.call-update) | async-done | bytes 2097168 | tf_op jit(solution)/shard_map/psum | solution.py:16
  449.5 3.6 fusion.1
  455.5 3.2 fusion
  458.7 3.2 fusion.2
  462.8 2.4 copy-done.4
  466.5 3.2 fusion.5
  469.7 2.6 fusion.6
  472.3 3.6 copy.38
  475.9 7.1 %fusion.7 = bf16[32,32,256]{0,1,2:T(8,128)(2,1)S(1)} fusion(bf16[2,32,32,256]{2,1,3,0:T(8,128)(2,1)} %copy-done.2, bf16[2,32,32,256]{2,1,3,0:T(8,128)(2,1)} %get-tuple-element.9, f32[256,32,32]{2,1,0:T(8,128)} %fusion.5, f32[256,32,32]{2,1,0:T(8,128)} %fusion.2, f32[256,32,32]{2,1,0:T(8,128)} %fusion), kind=kOutput, calls=%fused_computation.28 | convolution fusion | flops 17825792 | bytes 17301504 | tf_op jit(solution)/shard_map/spf,prf->srf/dot_general | solution.py:60
  483.0 2.1 copy.39
  485.3 3.9 multiply_convert_fusion.2
  (33 shorter events, 7.5 us)
Async XLA Ops:
  6.5 7.5 %copy-start = (bf16[2,32,32,256]{3,2,1,0:T(8,128)(2,1)S(1)}, bf16[2,32,32,256]{3,2,1,0:T(8,128)(2,1)}, u32[]{:S(2)}) copy-start(bf16[2,32,32,256]{3,2,1,0:T(8,128)(2,1)} %param.8) | copy-start | bytes 3145732
  6.5 242.5 %all-reduce.5.cloned.1.call-start = ((), (), s32[]{:S(2)}) async-start(), calls=%async_computation | async-start | bytes 16777216 | tf_op jit(solution)/shard_map/psum | solution.py:16
  40.2 409.4 %all-reduce.7.cloned.1.call-start = ((), (), s32[]{:S(2)}) async-start(), calls=%async_computation.1 | async-start | bytes 16777216 | tf_op jit(solution)/shard_map/psum | solution.py:16
  60.9 0.7 copy-start.8
  60.9 0.7 copy-start.7
  449.5 3.6 copy-start.3
  449.5 4.7 copy-start.5
  458.7 3.2 copy-start.6
  461.9 3.3 copy-start.4
  462.8 6.9 %copy-start.2 = (bf16[2,32,32,256]{2,1,3,0:T(8,128)(2,1)}, bf16[2,32,32,256]{2,1,3,0:T(8,128)(2,1)S(1)}, u32[]{:S(2)}) copy-start(bf16[2,32,32,256]{2,1,3,0:T(8,128)(2,1)S(1)} %multiply_convert_fusion) | copy-start | bytes 3145732
  485.3 3.9 copy-start.1
Sparse Core Ops, SparseCore 0:
  40.3 208.7 all-reduce.4
  251.8 197.6 all-reduce.6
where the time goes:
time: 496 us
  waiting for transfers between devices  373 us (75%)
  local copies, waits for them, and re-layouts  45.6 us (9%)
  matrix products  29.4 us (6%)
  other arithmetic  28.5 us (6%)
  between operations  18.9 us (4%)
    psum x2, waiting for transfers between devices, spread(): return lax.psum(block, axis)  373 us
    gather x4, local copies, waits for them, and re-layouts, body(): picked = jnp.take(data, local_cols, axis=2)  20.1 us
    gather x4, local copies, waits for them, and re-layouts, body(): right_panel = spread(jnp.take(data, local_rows, axis=1), 'src', owner_src)  14.2 us
    select_n x2, other arithmetic, spread(): jnp.where(lax.axis_index(axis) == holder, block, jnp.zeros_like(block))  12.2 us
    dot_general x2, matrix products, body(): jnp.einsum(product_form, weighted[1], right_panel[0], preferred_element_t...  10.3 us
  transfers between devices with their start and end apart: 2, of which 2 were waited for; matrix products, arithmetic and copies ran while one was open for 7% of the time, Pallas kernels for 0%

commit v1 on v0

v1 whole, which is shorter than its diff:
```python
import functools
import math

import jax
import jax.numpy as jnp
from jax import lax
from jax.experimental import pallas as pl
from jax.experimental.pallas import tpu as pltpu
from jax.sharding import PartitionSpec as P

NF = 256
NT = 1024
PANEL = 32
STEPS = 2
BLK = 32
LANES = 128
HALF = 64
CH = 4
NCH = 8
SLOPE = 3
LAG = 3
MESH = pl.DeviceIdType.MESH


def device(x, lo, core, h, z):
    return (x * 4 + lo * 2 + core, h * 8 + z)


def here():
    src = lax.axis_index("src")
    rcv = lax.axis_index("rcv")
    return src // 4, (src // 2) % 2, src % 2, rcv // 8, rcv % 8


def after(depth):
    return (depth * SLOPE) // 2


def gather_kernel(
    data, weight, band, z_out, table,
    turned, left, right, spec_out, spec_in,
    l_send, l_recv, r_send, r_recv, s_send, s_recv,
):
    x, lo, core, h, z = here()
    other = 1 - h

    barrier = pltpu.get_barrier_semaphore()
    neighbours = [
        device(x, lo, core, h, (z + 1) % 8),
        device(x, lo, core, h, (z + 7) % 8),
        device(x, lo, core, other, z),
        device(x, 1 - lo, core, h, z),
        device((x + 1) % 4, lo, core, h, z),
        device((x + 3) % 4, lo, core, h, z),
        device(x, lo, 1 - core, h, z),
    ]
    for one in neighbours:
        pl.semaphore_signal(barrier, inc=1, device_id=one, device_id_type=MESH)

    seen = [(x, lo, core, h, z), (3 - x, 1 - lo, 1 - core, 1 - h, 7 - z)]
    step = [1, -1]

    for g in range(2):
        xm, lm, cm, hm, zm = seen[g]

        @pl.when((hm == 0) & (zm == 0))
        def _():
            scale = weight[g]

            @pl.loop(0, BLK, unroll=2)
            def _(s):
                rows = jnp.concatenate(
                    [
                        (
                            data[c, s, :, fh * LANES : (fh + 1) * LANES].astype(
                                jnp.float32
                            )
                            * scale
                        )
                        .astype(jnp.bfloat16)
                        .astype(jnp.float32)
                        for fh in range(2)
                        for c in range(2)
                    ],
                    axis=0,
                )
                turned[pl.ds(s, LANES, stride=BLK), :] = rows.T

            @pl.loop(0, LANES, unroll=4)
            def _(f):
                left[g, f] = turned[pl.ds(f * BLK, BLK), :].astype(jnp.bfloat16)

        @pl.when((xm == 0) & (lm == 0) & (cm == 0))
        def _():
            @pl.loop(0, BLK, unroll=2)
            def _(q):
                rows = jnp.concatenate(
                    [
                        data[c, q, :, fh * LANES : (fh + 1) * LANES].astype(jnp.float32)
                        for c in range(2)
                        for fh in range(2)
                    ],
                    axis=0,
                )
                turned[pl.ds(q, LANES, stride=BLK), :] = rows.T

            @pl.loop(0, LANES, unroll=4)
            def _(f):
                right[g, 0, f // HALF, (f // BLK) % 2, f % BLK] = turned[
                    pl.ds(f * BLK, BLK), :
                ].astype(jnp.bfloat16)

    pl.semaphore_wait(barrier, len(neighbours))

    def left_copy(g, d, k, row, slot, target):
        start = row * HALF + d * BLK + k * CH
        ref = left.at[g, pl.ds(start, CH)]
        return pltpu.make_async_remote_copy(
            src_ref=ref, dst_ref=ref,
            send_sem=l_send.at[g, d, k, slot], recv_sem=l_recv.at[g, d, k],
            device_id=target, device_id_type=MESH,
        )

    def right_copy(g, rel, k, row, slot, target, cross=False):
        return pltpu.make_async_remote_copy(
            src_ref=right.at[g, 0 if cross else rel, row, :, pl.ds(k * CH, CH)],
            dst_ref=right.at[g, rel, row, :, pl.ds(k * CH, CH)],
            send_sem=r_send.at[g, rel, k, slot], recv_sem=r_recv.at[g, rel, k],
            device_id=target, device_id_type=MESH,
        )

    def spec_copy(d, k):
        return pltpu.make_async_remote_copy(
            src_ref=spec_out.at[d, pl.ds(k * CH, CH)],
            dst_ref=spec_in.at[d, pl.ds(k * CH, CH)],
            send_sem=s_send.at[d, k], recv_sem=s_recv.at[d, k],
            device_id=device(x, lo, core, other, z), device_id_type=MESH,
        )

    def left_plan(g, d):
        _, _, _, hm, zm = seen[g]
        pos = zm if d == 0 else (8 - zm) % 8
        along = step[g] if d == 0 else -step[g]
        onward = device(x, lo, core, h, (z + along + 8) % 8)
        return pos, pos + hm, (pos == 0) & (hm == 0), onward

    def right_plan(g, rel):
        xm, lm, cm, _, _ = seen[g]
        first = jnp.where(xm == 3, 1, xm)
        root = (xm == 0) & (lm == 0) & (cm == 0)
        return xm, lm, cm, root, rel + lm + first + cm

    def right_sends(g, rel):
        xm, lm, cm, root, _ = right_plan(g, rel)
        up, down = (x + step[g] + 4) % 4, (x - step[g] + 4) % 4
        return [
            (cm == 0, device(x, lo, 1 - core, h, z)),
            ((cm == 0) & (xm == 0) & (lm == 0), device(x, 1 - lo, core, h, z)),
            ((cm == 0) & (xm <= 1), device(up, lo, core, h, z)),
            ((cm == 0) & (xm == 0), device(down, lo, core, h, z)),
        ]

    partner = device(x, lo, core, other, z)
    reach = []
    reach_other = []
    for d in range(2):
        mine = theirs = jnp.int32(0)
        for g in range(2):
            pos, depth, _, _ = left_plan(g, d)
            mine = jnp.maximum(mine, depth)
            theirs = jnp.maximum(theirs, pos + (1 - seen[g][3]))
            right_depth = right_plan(g, 1)[4]
            mine = jnp.maximum(mine, right_depth)
            theirs = jnp.maximum(theirs, right_depth)
        reach.append(after(mine))
        reach_other.append(after(jnp.maximum(mine, theirs)) + LAG)

    lane = lax.broadcasted_iota(jnp.int32, (BLK, LANES), 1)
    in_half = [(lane // BLK) % 2 == fh for fh in range(2)]
    keep = [jnp.where(m, 1.0, 0.0).astype(jnp.bfloat16) for m in in_half]
    sign = [
        jnp.where(m, jnp.where(lane < HALF, -1.0, 1.0), 0.0).astype(jnp.bfloat16)
        for m in in_half
    ]

    def spectra(d, k):
        @pl.loop(0, CH, unroll=True)
        def _(i):
            f = h * HALF + d * BLK + k * CH + i
            rows = jnp.concatenate([left[0, f], left[1, f]], axis=1)
            columns = []
            for rel in range(2):
                parts = []
                for g in range(2):
                    held = right[g, rel, h, d, k * CH + i]
                    swapped = jnp.concatenate([held[:, HALF:], held[:, :HALF]], axis=1)
                    for fh in range(2):
                        parts += [held * keep[fh], swapped * sign[fh]]
                columns.append(jnp.concatenate(parts, axis=0))
            product = jnp.dot(
                rows,
                jnp.concatenate(columns, axis=1),
                preferred_element_type=jnp.float32,
            )
            z_out[pl.ds(f, BLK, stride=LANES), :] = product[:, :LANES]
            spec_out[d, k * CH + i] = product[:, LANES:].astype(jnp.bfloat16)

        spec_copy(d, k).start()

    def take_in(d, k):
        spec_copy(d, k).wait_recv()

        @pl.loop(0, CH, unroll=True)
        def _(i):
            f = other * HALF + d * BLK + k * CH + i
            z_out[pl.ds(f, BLK, stride=LANES), :] = spec_in[d, k * CH + i].astype(
                jnp.float32
            )

    def within(k):
        return (k >= 0) & (k < NCH)

    slots = NCH + after(8) + LAG

    @pl.loop(0, slots)
    def _(t):
        for g in range(2):
            for d in range(2):
                pos, depth, source, onward = left_plan(g, d)
                k = t - after(depth)

                @pl.when(within(k))
                def _():
                    own = left_copy(g, d, k, h, 0, onward)

                    @pl.when(jnp.logical_not(source))
                    def _():
                        own.wait_recv()

                    @pl.when(pos < 7)
                    def _():
                        own.start()

                    @pl.when(source)
                    def _():
                        left_copy(g, d, k, other, 1, partner).start()

            for rel in range(2):
                xm, lm, cm, root, depth = right_plan(g, rel)
                k = t - after(depth)

                @pl.when(within(k))
                def _():
                    awaited = jnp.logical_not(root) if rel == 0 else root | True

                    @pl.when(awaited)
                    def _():
                        right_copy(g, rel, k, h, 0, partner).wait_recv()

                    for slot, (sends, target) in enumerate(right_sends(g, rel)):

                        @pl.when(sends)
                        def _():
                            right_copy(g, rel, k, h, slot, target).start()

                    if rel == 0:

                        @pl.when(root)
                        def _():
                            right_copy(g, 1, k, other, 4, partner, True).start()

        for d in range(2):
            k = t - reach[d]

            @pl.when(within(k))
            def _():
                spectra(d, k)

            k_in = t - reach_other[d]

            @pl.when(within(k_in))
            def _():
                take_in(d, k_in)

        if True:

            @pl.when(t == 0)
            def _():
                turns = jnp.float32(2.0 * math.pi / NT)
                bins = band[...]
                sample = lax.broadcasted_iota(jnp.int32, (NF, LANES), 1)
                fine = ((bins * sample) & (NT - 1)).astype(jnp.float32) * turns
                cos_fine, sin_fine = jnp.cos(fine), jnp.sin(fine)
                for block in range(NT // LANES):
                    coarse = ((bins * (block * LANES)) & (NT - 1)).astype(
                        jnp.float32
                    ) * turns
                    cos_coarse, sin_coarse = jnp.cos(coarse), jnp.sin(coarse)
                    at = slice(block * LANES, (block + 1) * LANES)
                    table[:NF, at] = (
                        cos_coarse * cos_fine - sin_coarse * sin_fine
                    ).astype(jnp.bfloat16)
                    table[NF:, at] = (
                        -(sin_coarse * cos_fine + cos_coarse * sin_fine)
                    ).astype(jnp.bfloat16)

    @pl.loop(0, NCH)
    def _(k):
        for d in range(2):
            spec_copy(d, k).wait_send()
            for g in range(2):
                pos, _, source, onward = left_plan(g, d)

                @pl.when(pos < 7)
                def _():
                    left_copy(g, d, k, h, 0, onward).wait_send()

                @pl.when(source)
                def _():
                    left_copy(g, d, k, other, 1, partner).wait_send()

        for g in range(2):
            for rel in range(2):
                for slot, (sends, target) in enumerate(right_sends(g, rel)):

                    @pl.when(sends)
                    def _():
                        right_copy(g, rel, k, h, slot, target).wait_send()

            @pl.when(right_plan(g, 0)[3])
            def _():
                right_copy(g, 1, k, other, 4, partner, True).wait_send()


def gathered_spectra(data, weight, band):
    vmem = pl.BlockSpec(memory_space=pltpu.VMEM)
    dma = pltpu.SemaphoreType.DMA
    bf16 = jnp.bfloat16
    return pl.pallas_call(
        gather_kernel,
        out_shape=(
            jax.ShapeDtypeStruct((BLK * LANES, LANES), jnp.float32),
            jax.ShapeDtypeStruct((2 * NF, NT), bf16),
        ),
        in_specs=[vmem] * 3,
        out_specs=(vmem, vmem),
        scratch_shapes=[
            pltpu.VMEM((LANES * BLK, LANES), jnp.float32),
            pltpu.VMEM((2, LANES, BLK, LANES), bf16),
            pltpu.VMEM((2, 2, 2, 2, BLK, BLK, LANES), bf16),
            pltpu.VMEM((2, BLK, BLK, LANES), bf16),
            pltpu.VMEM((2, BLK, BLK, LANES), bf16),
            dma((2, 2, NCH, 2)),
            dma((2, 2, NCH)),
            dma((2, 2, NCH, 5)),
            dma((2, 2, NCH)),
            dma((2, NCH)),
            dma((2, NCH)),
        ],
        compiler_params=pltpu.CompilerParams(
            collective_id=0, has_side_effects=True, vmem_limit_bytes=40 * 2**20
        ),
        cost_estimate=pl.CostEstimate(
            flops=2 * HALF * BLK * 256 * 256,
            bytes_accessed=6 * 2**20,
            transcendentals=2 * NF * LANES,
        ),
        name="gathered_spectra",
    )(data, weight, band)


ROWS_AT_ONCE = 8


def to_time_kernel(scale, z_ref, table, out):
    rows = []
    for s in range(ROWS_AT_ONCE):
        turned = z_ref[s * LANES : (s + 1) * LANES, :].T.astype(jnp.bfloat16)
        rows.append(
            jnp.concatenate(
                [turned[j * BLK : (j + 1) * BLK, :] for j in range(4)], axis=1
            )
        )
    product = jnp.dot(
        jnp.concatenate(rows, axis=0), table[...], preferred_element_type=jnp.float32
    )
    out[...] = (product * scale).astype(jnp.bfloat16).reshape(ROWS_AT_ONCE, BLK, NT)


def to_time(z, table, scale):
    steps = BLK // ROWS_AT_ONCE
    return pl.pallas_call(
        functools.partial(to_time_kernel, scale),
        out_shape=jax.ShapeDtypeStruct((BLK, BLK, NT), jnp.bfloat16),
        grid=(steps,),
        in_specs=[
            pl.BlockSpec((ROWS_AT_ONCE * LANES, LANES), lambda i: (i, 0)),
            pl.BlockSpec((2 * NF, NT), lambda i: (0, 0)),
        ],
        out_specs=pl.BlockSpec((ROWS_AT_ONCE, BLK, NT), lambda i: (i, 0, 0)),
        compiler_params=pltpu.CompilerParams(vmem_limit_bytes=40 * 2**20),
        cost_estimate=pl.CostEstimate(
            flops=2 * 1024 * 512 * 1024, bytes_accessed=5 * 2**20, transcendentals=0
        ),
        name="to_time",
    )(z, table)


def body(data, panel_index, panel_weight, band_index):
    group_start = jnp.array([0, 512 - PANEL], jnp.int32)
    traces = group_start[:, None] + jnp.arange(PANEL, dtype=jnp.int32)[None, :]
    found = traces[:, :, None] == panel_index.reshape(-1)[None, None, :]
    weight = jnp.sum(
        jnp.where(found, panel_weight.reshape(-1)[None, None, :], 0.0), axis=2
    )
    weight = jnp.broadcast_to(weight[:, :, None], (2, PANEL, LANES))
    z, table = gathered_spectra(data, weight, band_index.reshape(NF, 1))
    norm_scale = 1.0 / math.sqrt(2.0 * STEPS * PANEL * NF)
    return to_time(z, table, -norm_scale)


def solution(mesh):
    placed = (P(None, "src", "rcv", None), P(), P(), P())
    return jax.shard_map(
        body, mesh=mesh, in_specs=placed, out_specs=P("src", "rcv", None), check_vma=False
    )
```

time: 496 us -> 80.2 us (0.16)
  the two profiles are of different devices: /device:TPU:5 before, /device:TPU:16 now
where the time goes in v1:
time: 80.2 us; the launch traced here: 80 us
  Pallas kernels  76.1 us (95%)
  local copies, waits for them, and re-layouts  3.63 us (5%)
    pallas_call x1, Pallas kernels, gathered_spectra(): pl.pallas_call(gather_kernel, out_shape=(jax.ShapeDtypeStruct((BLK * LANE...  73 us
    pallas_call x1, Pallas kernels, to_time(): pl.pallas_call(functools.partial(to_time_kernel, scale), out_shape=jax.Sh...  3.13 us

profile of v1, /device:TPU:16, one launch (start us, length us, event | category | flops | bytes accessed | tf_op | source)
XLA Modules:
  0.0 80.0 jit_solution(16999932086368428093)
XLA Ops:
  0.0 0.8 eq.16
  0.8 0.8 broadcast_in_dim.23
  1.5 0.1 iota_add_fusion
  1.6 0.2 select_reduce_fusion
  1.8 0.1 broadcast_in_dim.26.weight
  1.8 0.8 %copy.7.band = s32[256,1]{1,0:T(8,128)S(1)} copy(s32[256,1]{0,1:T(1,128)} %bitcast.1) | data formatting | bytes 2048 | tf_op jit(solution)/shard_map/reshape | solution.py:417
  2.7 0.0 copy-start
  2.7 1.2 %copy-done = bf16[2,32,32,256]{3,2,1,0:T(8,128)(2,1)S(1)} copy-done((bf16[2,32,32,256]{3,2,1,0:T(8,128)(2,1)S(1)}, bf16[2,32,32,256]{3,2,1,0:T(8,128)(2,1)}, u32[]{:S(2)}) %copy-start) | copy-done | bytes 1048600
  3.9 73.0 %gathered_spectra.1 = (f32[4096,128]{1,0:T(8,128)S(1)}, bf16[512,1024]{1,0:T(8,128)(2,1)S(1)}) custom-call(bf16[2,32,32,256]{3,2,1,0:T(8,128)(2,1)S(1)} %copy-done, f32[2,32,128]{2,1,0:T(8,128)S(1)} %broadcast_in_dim.26.weight, s32[256,1]{1,0:T(8,128)S(1)} %copy.7.band), custom_call_target="tpu_custom_call" | custom-call | flops 268435456 | bytes 6291456 | tf_op jit(solution)/shard_map/gathered_spectra/pallas_call | solution.py:339
  76.9 3.1 %to_time.1 = bf16[32,32,1024]{2,1,0:T(8,128)(2,1)} custom-call(f32[4096,128]{1,0:T(8,128)S(1)} %get-tuple-element.7.z_ref, bf16[512,1024]{1,0:T(8,128)(2,1)S(1)} %get-tuple-element.8.table), custom_call_target="tpu_custom_call" | custom-call | flops 1073741824 | bytes 5242880 | tf_op jit(solution)/shard_map/to_time/pallas_call | solution.py:392
  (1 shorter events, 0.0 us)
Async XLA Ops:
  2.7 1.2 %copy-start = (bf16[2,32,32,256]{3,2,1,0:T(8,128)(2,1)S(1)}, bf16[2,32,32,256]{3,2,1,0:T(8,128)(2,1)}, u32[]{:S(2)}) copy-start(bf16[2,32,32,256]{3,2,1,0:T(8,128)(2,1)} %data.1) | copy-start | bytes 3145732

commit v2 on v0

v2 whole, which is shorter than its diff:
```python
import functools
import math

import jax
import jax.numpy as jnp
from jax import lax
from jax.experimental import pallas as pl
from jax.experimental.pallas import tpu as pltpu
from jax.sharding import PartitionSpec as P

NF = 256
NT = 1024
PANEL = 32
STEPS = 2
BLK = 32
LANES = 128
HALF = 64
CH = 4
MESH = pl.DeviceIdType.MESH


def device(x, lo, core, h, z):
    return (x * 4 + lo * 2 + core, h * 8 + z)


def here():
    src = lax.axis_index("src")
    rcv = lax.axis_index("rcv")
    return src // 4, (src // 2) % 2, src % 2, rcv // 8, rcv % 8


def gather_kernel(
    data_hbm, index_hbm, weight_hbm, band_hbm, z_out, table,
    data, panel_index, panel_weight, band, turned, left, right, spec_out, spec_in,
    data_sem, small_sem, l_recv, l_first, l_send, r_recv, r_first, r_send, r_side,
    s_send, s_recv,
):
    x, lo, core, h, z = here()
    other = 1 - h
    partner = device(x, lo, core, other, z)
    sibling = device(x, lo, 1 - core, h, z)
    l_source = [(h == g) & (z == 7 * g) for g in range(2)]
    root = (x == 3 * core) & (lo == core)
    any_source = l_source[0] | l_source[1]

    def z_off(dz):
        return (z + dz + 8) % 8

    def x_off(dx):
        return (x + dx) % 4

    @pl.when(any_source | root)
    def _():
        pltpu.make_async_copy(data_hbm, data, data_sem).start()

    small = [
        pltpu.make_async_copy(src, dst, small_sem.at[i])
        for i, (src, dst) in enumerate(
            ((index_hbm, panel_index), (weight_hbm, panel_weight), (band_hbm, band))
        )
    ]
    for one in small:
        one.start()

    barrier = pltpu.get_barrier_semaphore()

    def arrive(target):
        pl.semaphore_signal(barrier, inc=1, device_id=target, device_id_type=MESH)

    for dz in (1, -1, 2, -2):
        arrive(device(x, lo, core, h, z_off(dz)))
    for dx in (1, 2, 3):
        arrive(device(x_off(dx), lo, core, h, z))
    arrive(sibling)
    arrive(partner)
    for g in range(2):

        @pl.when(jnp.logical_not(l_source[g]))
        def _():
            arrive(device(x, lo, core, g, 7 * g))

    for row in range(2):

        @pl.when(jnp.logical_not(root & (h == row)))
        def _():
            arrive(device(3 * core, core, core, row, z))

    for one in small:
        one.wait()

    @pl.when(any_source | root)
    def _():
        pltpu.make_async_copy(data_hbm, data, data_sem).wait()

    def turn(block_rows, store):
        @pl.loop(0, BLK, unroll=2)
        def _(s):
            turned[pl.ds(s, LANES, stride=BLK), :] = block_rows(s).T

        @pl.loop(0, 2 * HALF, unroll=4)
        def _(f):
            store(f, turned[pl.ds(f * BLK, BLK), :].astype(jnp.bfloat16))

    for g in range(2):

        @pl.when(l_source[g])
        def _():
            trace = lax.broadcasted_iota(jnp.int32, (BLK, PANEL), 0) + g * (512 - PANEL)
            scale = jnp.zeros((BLK, 1), jnp.float32)
            for t in range(STEPS):
                found = trace == panel_index[t : t + 1, :]
                scale = scale + jnp.sum(
                    jnp.where(found, panel_weight[t : t + 1, :], 0.0),
                    axis=1,
                    keepdims=True,
                )
            scale = jnp.broadcast_to(scale, (BLK, LANES))

            def block_rows(s):
                parts = []
                for fh in range(2):
                    for c in range(2):
                        part = data[c, s, :, fh * LANES : (fh + 1) * LANES]
                        part = (part.astype(jnp.float32) * scale).astype(jnp.bfloat16)
                        parts.append(part.astype(jnp.float32))
                return jnp.concatenate(parts, axis=0)

            def store(f, value):
                left[g, f // HALF, (f // BLK) % 2, (f // CH) % 8, f % CH] = value

            turn(block_rows, store)

    @pl.when(root)
    def _():
        def block_rows(q):
            return jnp.concatenate(
                [
                    data[c, q, :, fh * LANES : (fh + 1) * LANES].astype(jnp.float32)
                    for c in range(2)
                    for fh in range(2)
                ],
                axis=0,
            )

        def store(f, value):
            right[core, 0, f // HALF, (f // BLK) % 2, (f // 8) % 4, f % 8] = value

        turn(block_rows, store)

    incoming = 9 + 15 * (
        any_source.astype(jnp.int32) + root.astype(jnp.int32)
    )
    pl.semaphore_wait(barrier, incoming)

    def copy(src, dst, send, recv, target):
        return pltpu.make_async_remote_copy(
            src_ref=src, dst_ref=dst, send_sem=send, recv_sem=recv,
            device_id=target, device_id_type=MESH,
        )

    def first_left(g, row, p, u):
        ref = left.at[g, row, u, p]
        return copy(
            ref, ref, l_first.at[row, p, u], l_recv.at[g, p, u],
            device(x, lo, core, row, p),
        )

    def left_copy(g, p, u, slot, to_z):
        ref = left.at[g, h, u, p]
        return copy(
            ref, ref, l_send.at[g, u, slot], l_recv.at[g, p, u],
            device(x, lo, core, h, to_z),
        )

    def left_sends(g, u, level):
        if level == 1:
            return [(z, i, z_off(dz)) for i, dz in enumerate((2, -2, 1, -1))]
        return [
            (z_off(2), 4, z_off(-1)),
            (z_off(-2), 5, z_off(1)),
            (z_off(-2), 6, z_off(2)) if u == 0 else (z_off(2), 6, z_off(-2)),
        ]

    def send_left(g, u, level, wait=False):
        for p, slot, to_z in left_sends(g, u, level):

            @pl.when(jnp.logical_not((h == g) & (to_z == 7 * g)))
            def _():
                one = left_copy(g, p, u, slot, to_z)
                if wait:
                    one.wait_send()
                else:
                    one.start()

    def await_left(g, p, u):
        @pl.when(jnp.logical_not(l_source[g]))
        def _():
            left_copy(g, p, u, 0, z_off(1)).wait_recv()

    def first_right(row, part, to_lo, u):
        rel = jnp.where(row == h, 0, 1)
        return copy(
            right.at[core, 0, row, u, part], right.at[core, rel, row, u, part],
            r_first.at[row, part, to_lo, u], r_recv.at[core, rel, part, u],
            device(part, to_lo, core, row, z),
        )

    def right_copy(g, rel, part, u, send, target):
        ref = right.at[g, rel, h, u, part]
        return copy(ref, ref, send, r_recv.at[g, rel, part, u], target)

    def across_right(rel, u, dx):
        return right_copy(
            core, rel, x, u, r_send.at[rel, u, dx], device(x_off(dx), lo, core, h, z)
        )

    def across_allowed(rel, dx):
        to_root = (x_off(dx) == 3 * core) & (lo == core)
        return jnp.logical_not(to_root) if rel == 0 else to_root | True

    def side_right(rel, part, u):
        return right_copy(core, rel, part, u, r_side.at[rel, part, u], sibling)

    def await_right(rel, part, u):
        def wait():
            right_copy(core, rel, part, u, r_side.at[0, 0, 0], sibling).wait_recv()

        if rel == 0:
            pl.when(jnp.logical_not(root))(wait)
        else:
            wait()

    def spec_copy(p, u):
        return copy(
            spec_out.at[u, p], spec_in.at[u, p], s_send.at[u, p], s_recv.at[u, p], partner
        )

    def scatter(u, wait=False):
        def act(one):
            if wait:
                one.wait_send()
            else:
                one.start()

        for g in range(2):

            @pl.when(l_source[g])
            def _():
                @pl.loop(0, 8)
                def _(i):
                    p = (z + i) % 8
                    act(first_left(g, other, p, u))

                    @pl.when(i > 0)
                    def _():
                        act(first_left(g, h, p, u))

        @pl.when(root)
        def _():
            @pl.loop(0, 4)
            def _(i):
                part = (x + i) % 4
                for to_lo in range(2):
                    act(first_right(other, part, to_lo, u))

                    @pl.when(jnp.logical_not((i == 0) & (lo == to_lo)))
                    def _():
                        act(first_right(h, part, to_lo, u))

    for u in range(2):
        scatter(u)

    fill_table(band, table)

    for u in range(2):
        for g in range(2):
            await_left(g, z, u)
            send_left(g, u, 1)
        for rel in range(2):
            await_right(rel, x, u)
            for dx in (2, 1, 3):

                @pl.when(across_allowed(rel, dx))
                def _():
                    across_right(rel, u, dx).start()

            side_right(rel, x, u).start()

    def pass_left_on(u):
        for g in range(2):
            await_left(g, z_off(2), u)
            await_left(g, z_off(-2), u)
            send_left(g, u, 2)

    def pass_right_on(u):
        for dx in (1, 3, 2):
            for rel in range(2):
                await_right(rel, x_off(dx), u)
                side_right(rel, x_off(dx), u).start()

    def await_side(u):
        for rel in range(2):
            for part in range(4):
                right_copy(
                    1 - core, rel, part, u, r_side.at[0, 0, 0], sibling
                ).wait_recv()

    lane = lax.broadcasted_iota(jnp.int32, (BLK, LANES), 1)
    in_half = [(lane // BLK) % 2 == fh for fh in range(2)]
    keep = [jnp.where(m, 1.0, 0.0).astype(jnp.bfloat16) for m in in_half]
    sign = [
        jnp.where(m, jnp.where(lane < HALF, -1.0, 1.0), 0.0).astype(jnp.bfloat16)
        for m in in_half
    ]

    def spectra(u, begin, end):
        @pl.loop(begin, end)
        def _(n):
            step = (n + 1) // 2
            p = (z + jnp.where(n % 2 == 1, step, 8 - step)) % 8

            @pl.when((n != 0) & (n != 3) & (n != 4))
            def _():
                for g in range(2):
                    await_left(g, p, u)

            for i in range(CH):
                f = h * HALF + u * BLK + p * CH + i
                rows = jnp.concatenate(
                    [left[0, h, u, p, i], left[1, h, u, p, i]], axis=1
                )
                columns = []
                for rel in range(2):
                    parts = []
                    for g in range(2):
                        held = right[g, rel, h, u, p // 2, (p % 2) * CH + i]
                        swapped = jnp.concatenate(
                            [held[:, HALF:], held[:, :HALF]], axis=1
                        )
                        for fh in range(2):
                            parts += [held * keep[fh], swapped * sign[fh]]
                    columns.append(jnp.concatenate(parts, axis=0))
                product = jnp.dot(
                    rows,
                    jnp.concatenate(columns, axis=1),
                    preferred_element_type=jnp.float32,
                )
                z_out[pl.ds(f, BLK, stride=LANES), :] = product[:, :LANES]
                spec_out[u, p, i] = product[:, LANES:].astype(jnp.bfloat16)

            spec_copy(p, u).start()

    def take_in(u):
        @pl.loop(0, 8)
        def _(n):
            step = (n + 1) // 2
            p = (z + jnp.where(n % 2 == 1, step, 8 - step)) % 8
            spec_copy(p, u).wait_recv()
            for i in range(CH):
                f = other * HALF + u * BLK + p * CH + i
                z_out[pl.ds(f, BLK, stride=LANES), :] = spec_in[u, p, i].astype(
                    jnp.float32
                )

    pass_left_on(0)
    pass_right_on(0)
    await_side(0)
    spectra(0, 0, 5)
    pass_left_on(1)
    spectra(0, 5, 8)
    pass_right_on(1)
    await_side(1)
    spectra(1, 0, 8)
    take_in(0)
    take_in(1)

    for u in range(2):
        scatter(u, wait=True)
        for g in range(2):
            send_left(g, u, 1, wait=True)
            send_left(g, u, 2, wait=True)
        for rel in range(2):
            for dx in (1, 2, 3):

                @pl.when(across_allowed(rel, dx))
                def _():
                    across_right(rel, u, dx).wait_send()

            for part in range(4):
                side_right(rel, part, u).wait_send()

        @pl.loop(0, 8)
        def _(p):
            spec_copy(p, u).wait_send()


def fill_table(band, table):
    turns = jnp.float32(2.0 * math.pi / NT)
    bins = jnp.broadcast_to(band[...], (LANES, NF)).T
    sample = lax.broadcasted_iota(jnp.int32, (NF, LANES), 1)
    fine = ((bins * sample) & (NT - 1)).astype(jnp.float32) * turns
    cos_fine, sin_fine = jnp.cos(fine), jnp.sin(fine)
    root_half = jnp.float32(math.sqrt(0.5))
    for block in range(NT // LANES):
        eighth = (bins * block) & 7
        cos_coarse = eighth_cosine(eighth, root_half)
        sin_coarse = eighth_cosine((eighth + 6) & 7, root_half)
        at = slice(block * LANES, (block + 1) * LANES)
        table[:NF, at] = (cos_coarse * cos_fine - sin_coarse * sin_fine).astype(
            jnp.bfloat16
        )
        table[NF:, at] = (-(sin_coarse * cos_fine + cos_coarse * sin_fine)).astype(
            jnp.bfloat16
        )


def eighth_cosine(eighth, root_half):
    size = jnp.where(
        eighth % 2 == 1, root_half, jnp.where(eighth % 4 == 0, 1.0, 0.0)
    )
    return jnp.where((eighth >= 3) & (eighth <= 5), -size, size)


def gathered_spectra(data, panel_index, panel_weight, band):
    vmem = pl.BlockSpec(memory_space=pltpu.VMEM)
    dma = pltpu.SemaphoreType.DMA
    bf16 = jnp.bfloat16
    return pl.pallas_call(
        gather_kernel,
        out_shape=(
            jax.ShapeDtypeStruct((BLK * LANES, LANES), jnp.float32),
            jax.ShapeDtypeStruct((2 * NF, NT), bf16),
        ),
        in_specs=[pl.BlockSpec(memory_space=pltpu.HBM)] * 4,
        out_specs=(vmem, vmem),
        scratch_shapes=[
            pltpu.VMEM((2, BLK, BLK, NF), bf16),
            pltpu.VMEM((STEPS, PANEL), jnp.int32),
            pltpu.VMEM((STEPS, PANEL), jnp.float32),
            pltpu.VMEM((1, NF), jnp.int32),
            pltpu.VMEM((LANES * BLK, LANES), jnp.float32),
            pltpu.VMEM((2, 2, 2, 8, CH, BLK, LANES), bf16),
            pltpu.VMEM((2, 2, 2, 2, 4, 8, BLK, LANES), bf16),
            pltpu.VMEM((2, 8, CH, BLK, LANES), bf16),
            pltpu.VMEM((2, 8, CH, BLK, LANES), bf16),
            dma,
            dma((3,)),
            dma((2, 8, 2)),
            dma((2, 8, 2)),
            dma((2, 2, 7)),
            dma((2, 2, 4, 2)),
            dma((2, 4, 2, 2)),
            dma((2, 2, 4)),
            dma((2, 4, 2)),
            dma((2, 8)),
            dma((2, 8)),
        ],
        compiler_params=pltpu.CompilerParams(
            collective_id=0, has_side_effects=True, vmem_limit_bytes=40 * 2**20
        ),
        cost_estimate=pl.CostEstimate(
            flops=2 * HALF * BLK * 256 * 256,
            bytes_accessed=6 * 2**20,
            transcendentals=2 * NF * LANES,
        ),
        name="gathered_spectra",
    )(data, panel_index, panel_weight, band)


ROWS_AT_ONCE = 8


def to_time_kernel(scale, z_ref, table, out):
    rows = []
    for s in range(ROWS_AT_ONCE):
        turned = z_ref[s * LANES : (s + 1) * LANES, :].T.astype(jnp.bfloat16)
        rows.append(
            jnp.concatenate(
                [turned[j * BLK : (j + 1) * BLK, :] for j in range(4)], axis=1
            )
        )
    product = jnp.dot(
        jnp.concatenate(rows, axis=0), table[...], preferred_element_type=jnp.float32
    )
    out[...] = (product * scale).astype(jnp.bfloat16).reshape(ROWS_AT_ONCE, BLK, NT)


def to_time(z, table, scale):
    steps = BLK // ROWS_AT_ONCE
    return pl.pallas_call(
        functools.partial(to_time_kernel, scale),
        out_shape=jax.ShapeDtypeStruct((BLK, BLK, NT), jnp.bfloat16),
        grid=(steps,),
        in_specs=[
            pl.BlockSpec((ROWS_AT_ONCE * LANES, LANES), lambda i: (i, 0)),
            pl.BlockSpec((2 * NF, NT), lambda i: (0, 0)),
        ],
        out_specs=pl.BlockSpec((ROWS_AT_ONCE, BLK, NT), lambda i: (i, 0, 0)),
        compiler_params=pltpu.CompilerParams(vmem_limit_bytes=40 * 2**20),
        cost_estimate=pl.CostEstimate(
            flops=2 * 1024 * 512 * 1024, bytes_accessed=5 * 2**20, transcendentals=0
        ),
        name="to_time",
    )(z, table)


def body(data, panel_index, panel_weight, band_index):
    z, table = gathered_spectra(
        data, panel_index, panel_weight, band_index.reshape(1, NF)
    )
    norm_scale = 1.0 / math.sqrt(2.0 * STEPS * PANEL * NF)
    return to_time(z, table, -norm_scale)


def solution(mesh):
    placed = (P(None, "src", "rcv", None), P(), P(), P())
    return jax.shard_map(
        body, mesh=mesh, in_specs=placed, out_specs=P("src", "rcv", None), check_vma=False
    )
```

time: 496 us -> 57.9 us (0.12)
  waiting for transfers between devices: 373 us -> 0 us
  Pallas kernels: 0 us -> 53.4 us
  local copies, waits for them, and re-layouts: 45.6 us -> 3.26 us
  matrix products: 29.4 us -> 0 us
  other arithmetic: 28.5 us -> 0 us
  between operations: 18.9 us -> 0.01 us
    psum x2 -> x0, waiting for transfers between devices: 373 us -> none  [spread(): return lax.psum(block, axis)]
    pallas_call x0 -> x2, Pallas kernels: none -> 53.4 us  [the longest x1 50.3 us: gathered_spectra(): pl.pallas_call(gather_kernel, out_shape=(jax.ShapeDtypeStruct((BLK * LANE...]
    gather x8 -> x0, local copies, waits for them, and re-layouts: 34.3 us -> none  [the longest x4 20.1 us: body(): picked = jnp.take(data, local_cols, axis=2)]
    dot_general x9 -> x0, matrix products: 29.4 us -> none  [the longest x2 10.3 us: body(): jnp.einsum(product_form, weighted[1], right_panel[0], preferred_element_t...]
    select_n x2 -> x0, other arithmetic: 12.2 us -> none  [spread(): jnp.where(lax.axis_index(axis) == holder, block, jnp.zeros_like(block))]
    convert_element_type x3 -> x0, other arithmetic: 10.6 us -> none  [the longest x2 5.76 us: body(): weighted = (columns.astype(jnp.float32) * panel_weight[step_index][None,...]
  transfers between devices with their start and end apart: 2 -> 0, of which waited for: 2 -> 0; matrix products, arithmetic and copies ran while one was open for 7% -> 0% of each run, Pallas kernels for 0% -> 0%
where the time goes in v2:
time: 57.9 us; the launch traced here: 56.7 us
  Pallas kernels  53.4 us (92%)
  local copies, waits for them, and re-layouts  3.26 us (6%)
    pallas_call x1, Pallas kernels, gathered_spectra(): pl.pallas_call(gather_kernel, out_shape=(jax.ShapeDtypeStruct((BLK * LANE...  50.3 us
    unnamed x8, local copies, waits for them, and re-layouts  3.26 us
    pallas_call x1, Pallas kernels, to_time(): pl.pallas_call(functools.partial(to_time_kernel, scale), out_shape=jax.Sh...  3.13 us

profile of v2, /device:TPU:5, one launch (start us, length us, event | category | flops | bytes accessed | tf_op | source)
XLA Modules:
  0.0 56.7 jit_solution(8555530575005663716)
XLA Ops:
  0.0 0.0 copy-start
  0.0 1.2 %copy-done = bf16[2,32,32,256]{3,2,1,0:T(8,128)(2,1)S(1)} copy-done((bf16[2,32,32,256]{3,2,1,0:T(8,128)(2,1)S(1)}, bf16[2,32,32,256]{3,2,1,0:T(8,128)(2,1)}, u32[]{:S(2)}) %copy-start) | copy-done | bytes 1048600
  1.2 0.0 copy-start.1
  1.2 0.7 %copy-done.1 = s32[2,32]{1,0:T(2,128)S(1)} copy-done((s32[2,32]{1,0:T(2,128)S(1)}, s32[2,32]{1,0:T(2,128)}, u32[]{:S(2)}) %copy-start.1) | copy-done | bytes 280
  1.9 0.0 copy-start.2
  1.9 0.7 %copy-done.2 = f32[2,32]{1,0:T(2,128)S(1)} copy-done((f32[2,32]{1,0:T(2,128)S(1)}, f32[2,32]{1,0:T(2,128)}, u32[]{:S(2)}) %copy-start.2) | copy-done | bytes 280
  2.6 0.0 copy-start.3
  2.6 0.7 %copy-done.3 = s32[256]{0:T(256)S(1)} copy-done((s32[256]{0:T(256)S(1)}, s32[256]{0:T(256)}, u32[]{:S(2)}) %copy-start.3) | copy-done | bytes 1048
  3.3 50.3 %gathered_spectra.1 = (f32[4096,128]{1,0:T(8,128)S(1)}, bf16[512,1024]{1,0:T(8,128)(2,1)S(1)}) custom-call(bf16[2,32,32,256]{3,2,1,0:T(8,128)(2,1)S(1)} %copy-done, s32[2,32]{1,0:T(2,128)S(1)} %copy-done.1, f32[2,32]{1,0:T(2,128)S(1)} %copy-done.2, s32[1,256]{1,0:T(1,128)S(1)} %bitcast.1), custom_call_target="tpu_custom_call" | custom-call | flops 268435456 | bytes 6291456 | tf_op jit(solution)/shard_map/gathered_spectra/pallas_call | solution.py:428
  53.6 3.1 %to_time.1 = bf16[32,32,1024]{2,1,0:T(8,128)(2,1)} custom-call(f32[4096,128]{1,0:T(8,128)S(1)} %get-tuple-element.7.z_ref, bf16[512,1024]{1,0:T(8,128)(2,1)S(1)} %get-tuple-element.8.table), custom_call_target="tpu_custom_call" | custom-call | flops 1073741824 | bytes 5242880 | tf_op jit(solution)/shard_map/to_time/pallas_call | solution.py:490
Async XLA Ops:
  0.0 1.2 %copy-start = (bf16[2,32,32,256]{3,2,1,0:T(8,128)(2,1)S(1)}, bf16[2,32,32,256]{3,2,1,0:T(8,128)(2,1)}, u32[]{:S(2)}) copy-start(bf16[2,32,32,256]{3,2,1,0:T(8,128)(2,1)} %data_hbm.1) | copy-start | bytes 3145732
  1.2 0.7 %copy-start.1 = (s32[2,32]{1,0:T(2,128)S(1)}, s32[2,32]{1,0:T(2,128)}, u32[]{:S(2)}) copy-start(s32[2,32]{1,0:T(2,128)} %index_hbm.1) | copy-start | bytes 772
  1.9 0.7 %copy-start.2 = (f32[2,32]{1,0:T(2,128)S(1)}, f32[2,32]{1,0:T(2,128)}, u32[]{:S(2)}) copy-start(f32[2,32]{1,0:T(2,128)} %weight_hbm.1) | copy-start | bytes 772
  2.6 0.7 %copy-start.3 = (s32[256]{0:T(256)S(1)}, s32[256]{0:T(256)}, u32[]{:S(2)}) copy-start(s32[256]{0:T(256)} %param.7) | copy-start | bytes 3076

commit v3 on v2

v3 whole, which is shorter than its diff:
```python
import functools
import math

import jax
import jax.numpy as jnp
from jax import lax
from jax.experimental import pallas as pl
from jax.experimental.pallas import tpu as pltpu
from jax.sharding import PartitionSpec as P

NF = 256
NT = 1024
PANEL = 32
STEPS = 2
BLK = 32
LANES = 128
HALF = 64
CH = 2
NU = 4
PER = HALF // NU
ROWS_AT_ONCE = 8
PARTS = 4
MESH = pl.DeviceIdType.MESH


def device(x, lo, core, h, z):
    return (x * 4 + lo * 2 + core, h * 8 + z)


def here():
    src = lax.axis_index("src")
    rcv = lax.axis_index("rcv")
    return src // 4, (src // 2) % 2, src % 2, rcv // 8, rcv % 8


def gather_kernel(
    data_hbm, small, z_out, table,
    data, turned, left, right, spec_out, spec_in,
    data_sem, l_own, l_past, l_first, l_send,
    r_own, r_rest, r_first, r_send, r_side_send, r_side, s_send, s_recv,
):
    x, lo, core, h, z = here()
    other = 1 - h
    partner = device(x, lo, core, other, z)
    sibling = device(x, lo, 1 - core, h, z)
    beside = device(x, 1 - lo, core, h, z)
    l_source = [(h == g) & (z == 7 * g) for g in range(2)]
    root = (x == 3 * core) & (lo == core)
    any_source = l_source[0] | l_source[1]

    def z_off(dz):
        return (z + dz + 8) % 8

    def x_off(dx):
        return (x + dx) % 4

    @pl.when(any_source | root)
    def _():
        pltpu.make_async_copy(data_hbm, data, data_sem).start()

    barrier = pltpu.get_barrier_semaphore()

    def arrive(target):
        pl.semaphore_signal(barrier, inc=1, device_id=target, device_id_type=MESH)

    for dz in (1, -1, 2, -2):
        arrive(device(x, lo, core, h, z_off(dz)))
    for dx in (1, 2, 3):
        arrive(device(x_off(dx), lo, core, h, z))
    arrive(sibling)
    arrive(partner)
    for g in range(2):

        @pl.when(jnp.logical_not(l_source[g]))
        def _():
            arrive(device(x, lo, core, g, 7 * g))

    for row in range(2):

        @pl.when((lo == core) & jnp.logical_not(root & (h == row)))
        def _():
            arrive(device(3 * core, core, core, row, z))

    @pl.when(lo != core)
    def _():
        arrive(beside)

    @pl.when(any_source | root)
    def _():
        pltpu.make_async_copy(data_hbm, data, data_sem).wait()

    def turn(block_rows, store):
        @pl.loop(0, BLK, unroll=2)
        def _(s):
            turned[pl.ds(s, LANES, stride=BLK), :] = block_rows(s).T

        @pl.loop(0, 2 * HALF, unroll=4)
        def _(f):
            store(f, turned[pl.ds(f * BLK, BLK), :].astype(jnp.bfloat16))

    for g in range(2):

        @pl.when(l_source[g])
        def _():
            trace = lax.broadcasted_iota(jnp.int32, (BLK, STEPS * PANEL), 0)
            trace = trace + g * (512 - PANEL)
            found = trace.astype(jnp.float32) == small[:, : STEPS * PANEL]
            scale = jnp.sum(
                jnp.where(found, small[:, STEPS * PANEL : LANES], 0.0),
                axis=1,
                keepdims=True,
            )
            scale = jnp.broadcast_to(scale, (BLK, LANES))

            def block_rows(s):
                parts = []
                for fh in range(2):
                    for c in range(2):
                        part = data[c, s, :, fh * LANES : (fh + 1) * LANES]
                        part = (part.astype(jnp.float32) * scale).astype(jnp.bfloat16)
                        parts.append(part.astype(jnp.float32))
                return jnp.concatenate(parts, axis=0)

            def store(f, value):
                left[g, f // HALF, (f // PER) % NU, (f // CH) % 8, f % CH] = value

            turn(block_rows, store)

    def turn_right():
        def block_rows(q):
            return jnp.concatenate(
                [
                    data[c, q, :, fh * LANES : (fh + 1) * LANES].astype(jnp.float32)
                    for c in range(2)
                    for fh in range(2)
                ],
                axis=0,
            )

        def store(f, value):
            right[core, 0, f // HALF, (f // PER) % NU, (f // (2 * CH)) % 4, f % (2 * CH)] = value

        turn(block_rows, store)

    pl.when(root & jnp.logical_not(any_source))(turn_right)

    incoming = (
        9
        + 15 * any_source.astype(jnp.int32)
        + 7 * root.astype(jnp.int32)
        + (lo == core).astype(jnp.int32)
    )
    pl.semaphore_wait(barrier, incoming)

    def copy(src, dst, send, recv, target):
        return pltpu.make_async_remote_copy(
            src_ref=src, dst_ref=dst, send_sem=send, recv_sem=recv,
            device_id=target, device_id_type=MESH,
        )

    def await_bytes(ref, sem):
        copy(ref, ref, sem, sem, partner).wait_recv()

    def first_left(g, row, p, u):
        ref = left.at[g, row, u, p]
        sem = l_first.at[jnp.where(row == h, 1, 0)]
        return copy(ref, ref, sem, l_own.at[g, u], device(x, lo, core, row, p))

    def left_sends(g, u, level):
        near, far = l_send.at[g, 0], l_send.at[g, 1]
        if level < 3:
            return [
                (z_off(-level), near, z_off(1)),
                (z_off(level), near, z_off(-1)),
            ]
        way = 1 if u % 2 == 0 else -1
        return [(z_off(-3 * way), far, z_off(way))]

    def send_left(g, u, level):
        for p, send, to_z in left_sends(g, u, level):

            @pl.when(jnp.logical_not((h == g) & (to_z == 7 * g)))
            def _():
                ref = left.at[g, h, u, p]
                recv = l_past.at[level, g, u]
                copy(ref, ref, send, recv, device(x, lo, core, h, to_z)).start()

    def await_left(g, u, count, sem):
        @pl.when(jnp.logical_not(l_source[g]))
        def _():
            await_bytes(left.at[g, h, u, pl.ds(0, count)], sem)

    def left_sent(g):
        beside_source = (h == g) & (z_off(1) == 7 * g)
        beside_source |= (h == g) & (z_off(-1) == 7 * g)
        for is_so, near, rounds in (
            (beside_source, 3, NU // 2),
            (jnp.logical_not(beside_source), 6, NU),
        ):

            @pl.when(is_so)
            def _():
                await_bytes(left.at[g, h, :, pl.ds(0, near)], l_send.at[g, 0])
                await_bytes(left.at[g, h, pl.ds(0, rounds), 0], l_send.at[g, 1])

    def first_right(row, part, u):
        rel = jnp.where(row == h, 0, 1)
        return copy(
            right.at[core, 0, row, u, part], right.at[core, rel, row, u, part],
            r_first.at[1 - rel], r_own.at[rel, u], device(part, lo, core, row, z),
        )

    def right_copy(rel, part, u, send, recv, target):
        ref = right.at[core, rel, h, u, part]
        return copy(ref, ref, send, recv, target)

    def across_right(rel, u, dx):
        return right_copy(
            rel, x, u, r_send.at[rel], r_rest.at[rel, u],
            device(x_off(dx), lo, core, h, z),
        )

    def beside_right(rel, u):
        return right_copy(rel, x, u, r_send.at[2], r_own.at[rel, u], beside)

    def across_allowed(rel, dx):
        to_root = (x_off(dx) == 3 * core) & (lo == core)
        return jnp.logical_not(to_root) if rel == 0 else to_root | True

    def side_right(rel, part, u):
        return right_copy(rel, part, u, r_side_send, r_side.at[u], sibling)

    def await_right(rel, u, count, sem):
        def wait():
            await_bytes(right.at[core, rel, h, u, pl.ds(0, count)], sem.at[rel, u])

        if rel == 0:
            pl.when(jnp.logical_not(root))(wait)
        else:
            wait()

    def spec_copy(p, u):
        return copy(
            spec_out.at[u, p], spec_in.at[u, p], s_send, s_recv.at[u], partner
        )

    def scatter_left(u):
        for g in range(2):

            @pl.when(l_source[g])
            def _():
                @pl.loop(0, 8)
                def _(i):
                    p = (z + i) % 8
                    first_left(g, other, p, u).start()

                    @pl.when(i > 0)
                    def _():
                        first_left(g, h, p, u).start()

    def scatter_right(u):
        @pl.when(root)
        def _():
            @pl.loop(0, 4)
            def _(i):
                part = (x + i) % 4
                first_right(other, part, u).start()

                @pl.when(i > 0)
                def _():
                    first_right(h, part, u).start()

    for u in range(NU):
        scatter_left(u)
    pl.when(root & any_source)(turn_right)
    for u in range(NU):
        scatter_right(u)

    fill_table(small, table)

    def begin_left(u):
        for g in range(2):
            await_left(g, u, 1, l_own.at[g, u])
            send_left(g, u, 0)

    def begin_right(u):
        for rel in range(2):
            await_right(rel, u, 1, r_own)

            @pl.when(lo == core)
            def _():
                beside_right(rel, u).start()

            for dx in (2, 1, 3):

                @pl.when(across_allowed(rel, dx))
                def _():
                    across_right(rel, u, dx).start()

            side_right(rel, x, u).start()

    def pass_left_on(u, level):
        for g in range(2):
            await_left(g, u, 2, l_past.at[level - 1, g, u])
            send_left(g, u, level)

    def pass_right_on(u):
        for rel in range(2):
            await_right(rel, u, 3, r_rest)
            for dx in (1, 2, 3):
                side_right(rel, x_off(dx), u).start()

    def await_side(u):
        await_bytes(right.at[1 - core, :, h, u], r_side.at[u])

    lane = lax.broadcasted_iota(jnp.int32, (BLK, LANES), 1)
    in_half = [(lane // BLK) % 2 == fh for fh in range(2)]
    keep = [jnp.where(m, 1.0, 0.0).astype(jnp.bfloat16) for m in in_half]
    sign = [
        jnp.where(m, jnp.where(lane < HALF, -1.0, 1.0), 0.0).astype(jnp.bfloat16)
        for m in in_half
    ]

    def spectra(u):
        @pl.loop(0, 8)
        def _(p):

            for i in range(CH):
                f = h * HALF + u * PER + p * CH + i
                rows = jnp.concatenate(
                    [left[0, h, u, p, i], left[1, h, u, p, i]], axis=1
                )
                columns = []
                for rel in range(2):
                    parts = []
                    for g in range(2):
                        held = right[g, rel, h, u, p // 2, (p % 2) * CH + i]
                        swapped = jnp.concatenate(
                            [held[:, HALF:], held[:, :HALF]], axis=1
                        )
                        for fh in range(2):
                            parts += [held * keep[fh], swapped * sign[fh]]
                    columns.append(jnp.concatenate(parts, axis=0))
                product = jnp.dot(
                    rows,
                    jnp.concatenate(columns, axis=1),
                    preferred_element_type=jnp.float32,
                )
                z_out[pl.ds(f, BLK, stride=LANES), :] = product[:, :LANES]
                spec_out[u, p, i] = product[:, LANES:].astype(jnp.bfloat16)

            spec_copy(p, u).start()

    def take_in(u):
        await_bytes(spec_in.at[u], s_recv.at[u])

        @pl.loop(0, 8)
        def _(p):
            for i in range(CH):
                f = other * HALF + u * PER + p * CH + i
                z_out[pl.ds(f, BLK, stride=LANES), :] = spec_in[u, p, i].astype(
                    jnp.float32
                )

    def multiply(u):
        for g in range(2):
            await_left(g, u, 1, l_past.at[3, g, u])
        await_side(u)
        spectra(u)

    begin_left(0)
    begin_right(0)
    begin_left(1)
    begin_right(1)
    begin_left(2)
    pass_left_on(0, 1)
    begin_right(2)
    begin_left(3)
    pass_left_on(1, 1)
    begin_right(3)
    pass_left_on(2, 1)
    pass_left_on(0, 2)
    pass_right_on(0)
    pass_left_on(3, 1)
    pass_left_on(1, 2)
    pass_right_on(1)
    pass_left_on(2, 2)
    pass_left_on(0, 3)
    pass_left_on(3, 2)
    pass_left_on(1, 3)
    pass_right_on(2)
    pass_left_on(2, 3)
    multiply(0)
    pass_right_on(3)
    pass_left_on(3, 3)
    multiply(1)
    multiply(2)
    multiply(3)
    for u in range(NU):
        take_in(u)

    for g in range(2):

        @pl.when(l_source[g])
        def _():
            await_bytes(left.at[g, other], l_first.at[0])
            await_bytes(left.at[g, h, :, pl.ds(0, 7)], l_first.at[1])

        left_sent(g)

    @pl.when(root)
    def _():
        await_bytes(right.at[core, 0, other], r_first.at[0])
        await_bytes(right.at[core, 0, h, :, pl.ds(0, 3)], r_first.at[1])

    near_root = (lo == core) & jnp.logical_not(root)
    await_bytes(right.at[core, 1, h, :, pl.ds(0, 3)], r_send.at[1])

    @pl.when(near_root)
    def _():
        await_bytes(right.at[core, 0, h, :, pl.ds(0, 2)], r_send.at[0])

    @pl.when(jnp.logical_not(near_root))
    def _():
        await_bytes(right.at[core, 0, h, :, pl.ds(0, 3)], r_send.at[0])

    @pl.when(lo == core)
    def _():
        await_bytes(right.at[core, :, h, :, 0], r_send.at[2])

    await_bytes(right.at[core, :, h], r_side_send)
    await_bytes(spec_out, s_send)


def fill_table(small, table):
    turns = jnp.float32(2.0 * math.pi / NT)
    bins = jnp.broadcast_to(small[:, LANES:], (LANES, NF)).T.astype(jnp.int32)
    sample = lax.broadcasted_iota(jnp.int32, (NF, LANES), 1)
    fine = ((bins * sample) & (NT - 1)).astype(jnp.float32) * turns
    cos_fine, sin_fine = jnp.cos(fine), jnp.sin(fine)
    root_half = jnp.float32(math.sqrt(0.5))
    for block in range(NT // LANES):
        eighth = (bins * block) & 7
        cos_coarse = eighth_cosine(eighth, root_half)
        sin_coarse = eighth_cosine((eighth + 6) & 7, root_half)
        at = slice(block * LANES, (block + 1) * LANES)
        table[:NF, at] = (cos_coarse * cos_fine - sin_coarse * sin_fine).astype(
            jnp.bfloat16
        )
        table[NF:, at] = (-(sin_coarse * cos_fine + cos_coarse * sin_fine)).astype(
            jnp.bfloat16
        )


def eighth_cosine(eighth, root_half):
    size = jnp.where(
        eighth % 2 == 1, root_half, jnp.where(eighth % 4 == 0, 1.0, 0.0)
    )
    return jnp.where((eighth >= 3) & (eighth <= 5), -size, size)


def gathered_spectra(data, small):
    vmem = pl.BlockSpec(memory_space=pltpu.VMEM)
    dma = pltpu.SemaphoreType.DMA
    bf16 = jnp.bfloat16
    return pl.pallas_call(
        gather_kernel,
        out_shape=(
            jax.ShapeDtypeStruct((BLK * LANES, LANES), jnp.float32),
            jax.ShapeDtypeStruct((2 * NF, NT), bf16),
        ),
        in_specs=[pl.BlockSpec(memory_space=pl.ANY), vmem],
        out_specs=(vmem, vmem),
        scratch_shapes=[
            pltpu.VMEM((2, BLK, BLK, NF), bf16),
            pltpu.VMEM((LANES * BLK, LANES), jnp.float32),
            pltpu.VMEM((2, 2, NU, 8, CH, BLK, LANES), bf16),
            pltpu.VMEM((2, 2, 2, NU, PARTS, 2 * CH, BLK, LANES), bf16),
            pltpu.VMEM((NU, 8, CH, BLK, LANES), bf16),
            pltpu.VMEM((NU, 8, CH, BLK, LANES), bf16),
            dma,
            dma((2, NU)),
            dma((4, 2, NU)),
            dma((2,)),
            dma((2, 2)),
            dma((2, NU)),
            dma((2, NU)),
            dma((2,)),
            dma((3,)),
            dma,
            dma((NU,)),
            dma,
            dma((NU,)),
        ],
        compiler_params=pltpu.CompilerParams(
            collective_id=0, has_side_effects=True, vmem_limit_bytes=40 * 2**20
        ),
        cost_estimate=pl.CostEstimate(
            flops=2 * HALF * BLK * 256 * 256,
            bytes_accessed=4 * 2**20,
            transcendentals=2 * NF * LANES,
        ),
        name="gathered_spectra",
    )(data, small)


def to_time_kernel(scale, z_ref, table, out):
    rows = []
    for s in range(ROWS_AT_ONCE):
        turned = z_ref[s * LANES : (s + 1) * LANES, :].T.astype(jnp.bfloat16)
        rows.append(
            jnp.concatenate(
                [turned[j * BLK : (j + 1) * BLK, :] for j in range(4)], axis=1
            )
        )
    product = jnp.dot(
        jnp.concatenate(rows, axis=0), table[...], preferred_element_type=jnp.float32
    )
    out[...] = (product * scale).astype(jnp.bfloat16).reshape(ROWS_AT_ONCE, BLK, NT)


def to_time(z, table, scale):
    steps = BLK // ROWS_AT_ONCE
    return pl.pallas_call(
        functools.partial(to_time_kernel, scale),
        out_shape=jax.ShapeDtypeStruct((BLK, BLK, NT), jnp.bfloat16),
        grid=(steps,),
        in_specs=[
            pl.BlockSpec((ROWS_AT_ONCE * LANES, LANES), lambda i: (i, 0)),
            pl.BlockSpec((2 * NF, NT), lambda i: (0, 0)),
        ],
        out_specs=pl.BlockSpec((ROWS_AT_ONCE, BLK, NT), lambda i: (i, 0, 0)),
        compiler_params=pltpu.CompilerParams(vmem_limit_bytes=40 * 2**20),
        cost_estimate=pl.CostEstimate(
            flops=2 * 1024 * 512 * 1024, bytes_accessed=5 * 2**20, transcendentals=0
        ),
        name="to_time",
    )(z, table)


def body(data, panel_index, panel_weight, band_index):
    norm_scale = 1.0 / math.sqrt(2.0 * STEPS * PANEL * NF)
    small = jnp.concatenate(
        [
            panel_index.astype(jnp.float32).reshape(1, STEPS * PANEL),
            panel_weight.reshape(1, STEPS * PANEL),
            band_index.astype(jnp.float32).reshape(1, NF),
        ],
        axis=1,
    )
    z, table = gathered_spectra(data, small)
    return to_time(z, table, -norm_scale)


def solution(mesh):
    placed = (P(None, "src", "rcv", None), P(), P(), P())
    return jax.shard_map(
        body, mesh=mesh, in_specs=placed, out_specs=P("src", "rcv", None), check_vma=False
    )
```

time: 57.9 us -> 56.4 us (0.974)
  other arithmetic: 0 us -> 1.44 us
  Pallas kernels: 53.4 us -> 52 us
  local copies, waits for them, and re-layouts: 3.26 us -> 2.07 us
    unnamed x8 -> x2, local copies, waits for them, and re-layouts: 3.26 us -> 1.23 us
    pallas_call x1, Pallas kernels: 50.3 us -> 48.9 us  [gathered_spectra(): pl.pallas_call(gather_kernel, out_shape=(jax.ShapeDtypeStruct((BLK * LANE...]
    convert_element_type x0 -> x2, other arithmetic: none -> 1.36 us  [the longest x1 0.68 us: body(): panel_index.astype(jnp.float32).reshape(1, STEPS * PANEL)]
    reshape x0 -> x2, local copies, waits for them, and re-layouts: none -> 0.84 us  [the longest x1 0.76 us: body(): panel_weight.reshape(1, STEPS * PANEL)]
where the time goes in v3:
time: 56.4 us; the launch traced here: 55.6 us
  Pallas kernels  52 us (92%)
  local copies, waits for them, and re-layouts  2.07 us (4%)
  other arithmetic  1.44 us (3%)
    pallas_call x1, Pallas kernels, gathered_spectra(): pl.pallas_call(gather_kernel, out_shape=(jax.ShapeDtypeStruct((BLK * LANE...  48.9 us
    pallas_call x1, Pallas kernels, to_time(): pl.pallas_call(functools.partial(to_time_kernel, scale), out_shape=jax.Sh...  3.13 us
    unnamed x2, local copies, waits for them, and re-layouts  1.23 us

profile of v3, /device:TPU:5, one launch (start us, length us, event | category | flops | bytes accessed | tf_op | source)
XLA Modules:
  0.0 55.6 jit_solution(8317340150008796150)
XLA Ops:
  0.0 0.8 %reshape.10 = f32[1,64]{1,0:T(1,128)S(1)} reshape(f32[2,32]{1,0:T(2,128)} %param.6) | data formatting | bytes 512 | tf_op jit(solution)/shard_map/reshape | solution.py:546
  0.8 0.7 %convert_element_type.6 = f32[2,32]{1,0:T(2,128)S(1)} convert(s32[2,32]{1,0:T(2,128)} %param.5) | non-fusion elementwise | flops 64 | bytes 512 | tf_op jit(solution)/shard_map/convert_element_type | solution.py:545
  1.4 0.1 reshape.9
  1.5 0.7 %convert_element_type.7 = f32[256]{0:T(256)S(1)} convert(s32[256]{0:T(256)} %param.7) | non-fusion elementwise | flops 256 | bytes 2048 | tf_op jit(solution)/shard_map/convert_element_type | solution.py:547
  2.2 0.1 pad_maximum_fusion.small
  2.3 0.0 copy-start
  2.3 1.2 %copy-done = bf16[2,32,32,256]{3,2,1,0:T(8,128)(2,1)S(1)} copy-done((bf16[2,32,32,256]{3,2,1,0:T(8,128)(2,1)S(1)}, bf16[2,32,32,256]{3,2,1,0:T(8,128)(2,1)}, u32[]{:S(2)}) %copy-start) | copy-done | bytes 1048600
  3.5 48.9 %gathered_spectra.1 = (f32[4096,128]{1,0:T(8,128)S(1)}, bf16[512,1024]{1,0:T(8,128)(2,1)S(1)}) custom-call(bf16[2,32,32,256]{3,2,1,0:T(8,128)(2,1)S(1)} %copy-done, f32[1,384]{1,0:T(1,128)S(1)} %pad_maximum_fusion.small), custom_call_target="tpu_custom_call" | custom-call | flops 268435456 | bytes 4194304 | tf_op jit(solution)/shard_map/gathered_spectra/pallas_call | solution.py:466
  52.4 3.1 %to_time.1 = bf16[32,32,1024]{2,1,0:T(8,128)(2,1)} custom-call(f32[4096,128]{1,0:T(8,128)S(1)} %get-tuple-element.7.z_ref, bf16[512,1024]{1,0:T(8,128)(2,1)S(1)} %get-tuple-element.8.table), custom_call_target="tpu_custom_call" | custom-call | flops 1073741824 | bytes 5242880 | tf_op jit(solution)/shard_map/to_time/pallas_call | solution.py:524
Async XLA Ops:
  2.3 1.2 %copy-start = (bf16[2,32,32,256]{3,2,1,0:T(8,128)(2,1)S(1)}, bf16[2,32,32,256]{3,2,1,0:T(8,128)(2,1)}, u32[]{:S(2)}) copy-start(bf16[2,32,32,256]{3,2,1,0:T(8,128)(2,1)} %data_hbm.1) | copy-start | bytes 3145732

commit v4 on v3

--- a/solution.py
+++ b/solution.py
@@ -34,9 +34,9 @@
 
 
 def gather_kernel(
-    data_hbm, small, z_out, table,
-    data, turned, left, right, spec_out, spec_in,
-    data_sem, l_own, l_past, l_first, l_send,
+    data, panel_index, panel_weight, band, z_out, table,
+    turned, left, right, spec_out, spec_in,
+    l_own, l_past, l_first, l_send,
     r_own, r_rest, r_first, r_send, r_side_send, r_side, s_send, s_recv,
 ):
     x, lo, core, h, z = here()
@@ -54,10 +54,6 @@
     def x_off(dx):
         return (x + dx) % 4
 
-    @pl.when(any_source | root)
-    def _():
-        pltpu.make_async_copy(data_hbm, data, data_sem).start()
-
     barrier = pltpu.get_barrier_semaphore()
 
     def arrive(target):
@@ -85,10 +81,6 @@
     def _():
         arrive(beside)
 
-    @pl.when(any_source | root)
-    def _():
-        pltpu.make_async_copy(data_hbm, data, data_sem).wait()
-
     def turn(block_rows, store):
         @pl.loop(0, BLK, unroll=2)
         def _(s):
@@ -102,14 +94,15 @@
 
         @pl.when(l_source[g])
         def _():
-            trace = lax.broadcasted_iota(jnp.int32, (BLK, STEPS * PANEL), 0)
-            trace = trace + g * (512 - PANEL)
-            found = trace.astype(jnp.float32) == small[:, : STEPS * PANEL]
-            scale = jnp.sum(
-                jnp.where(found, small[:, STEPS * PANEL : LANES], 0.0),
-                axis=1,
-                keepdims=True,
-            )
+            trace = lax.broadcasted_iota(jnp.int32, (BLK, PANEL), 0) + g * (512 - PANEL)
+            scale = jnp.zeros((BLK, 1), jnp.float32)
+            for t in range(STEPS):
+                found = trace == panel_index[t : t + 1, :]
+                scale = scale + jnp.sum(
+                    jnp.where(found, panel_weight[t : t + 1, :], 0.0),
+                    axis=1,
+                    keepdims=True,
+                )
             scale = jnp.broadcast_to(scale, (BLK, LANES))
 
             def block_rows(s):
@@ -276,7 +269,7 @@
     for u in range(NU):
         scatter_right(u)
 
-    fill_table(small, table)
+    fill_table(band, table)
 
     def begin_left(u):
         for g in range(2):
@@ -432,9 +425,9 @@
     await_bytes(spec_out, s_send)
 
 
-def fill_table(small, table):
+def fill_table(band, table):
     turns = jnp.float32(2.0 * math.pi / NT)
-    bins = jnp.broadcast_to(small[:, LANES:], (LANES, NF)).T.astype(jnp.int32)
+    bins = jnp.broadcast_to(band[...], (LANES, NF)).T
     sample = lax.broadcasted_iota(jnp.int32, (NF, LANES), 1)
     fine = ((bins * sample) & (NT - 1)).astype(jnp.float32) * turns
     cos_fine, sin_fine = jnp.cos(fine), jnp.sin(fine)
@@ -459,7 +452,7 @@
     return jnp.where((eighth >= 3) & (eighth <= 5), -size, size)
 
 
-def gathered_spectra(data, small):
+def gathered_spectra(data, panel_index, panel_weight, band):
     vmem = pl.BlockSpec(memory_space=pltpu.VMEM)
     dma = pltpu.SemaphoreType.DMA
     bf16 = jnp.bfloat16
@@ -469,16 +462,14 @@
             jax.ShapeDtypeStruct((BLK * LANES, LANES), jnp.float32),
             jax.ShapeDtypeStruct((2 * NF, NT), bf16),
         ),
-        in_specs=[pl.BlockSpec(memory_space=pl.ANY), vmem],
+        in_specs=[vmem] * 4,
         out_specs=(vmem, vmem),
         scratch_shapes=[
-            pltpu.VMEM((2, BLK, BLK, NF), bf16),
             pltpu.VMEM((LANES * BLK, LANES), jnp.float32),
             pltpu.VMEM((2, 2, NU, 8, CH, BLK, LANES), bf16),
             pltpu.VMEM((2, 2, 2, NU, PARTS, 2 * CH, BLK, LANES), bf16),
             pltpu.VMEM((NU, 8, CH, BLK, LANES), bf16),
             pltpu.VMEM((NU, 8, CH, BLK, LANES), bf16),
-            dma,
             dma((2, NU)),
             dma((4, 2, NU)),
             dma((2,)),
@@ -501,7 +492,7 @@
             transcendentals=2 * NF * LANES,
         ),
         name="gathered_spectra",
-    )(data, small)
+    )(data, panel_index, panel_weight, band)
 
 
 def to_time_kernel(scale, z_ref, table, out):
@@ -540,15 +531,9 @@
 
 def body(data, panel_index, panel_weight, band_index):
     norm_scale = 1.0 / math.sqrt(2.0 * STEPS * PANEL * NF)
-    small = jnp.concatenate(
-        [
-            panel_index.astype(jnp.float32).reshape(1, STEPS * PANEL),
-            panel_weight.reshape(1, STEPS * PANEL),
-            band_index.astype(jnp.float32).reshape(1, NF),
-        ],
-        axis=1,
+    z, table = gathered_spectra(
+        data, panel_index, panel_weight, band_index.reshape(1, NF)
     )
-    z, table = gathered_spectra(data, small)
     return to_time(z, table, -norm_scale)
 
 

time: 56.4 us -> 55.9 us (level)
  other arithmetic: 1.44 us -> 0 us
  local copies, waits for them, and re-layouts: 2.07 us -> 3.26 us
    unnamed x2 -> x8, local copies, waits for them, and re-layouts: 1.23 us -> 3.26 us
    convert_element_type x2 -> x0, other arithmetic: 1.36 us -> none  [the longest x1 0.68 us: body(): panel_index.astype(jnp.float32).reshape(1, STEPS * PANEL)]
    reshape x2 -> x0, local copies, waits for them, and re-layouts: 0.84 us -> none  [the longest x1 0.76 us: body(): panel_weight.reshape(1, STEPS * PANEL)]
where the time goes in v4:
time: 55.9 us; the launch traced here: 55.1 us
  Pallas kernels  51.8 us (93%)
  local copies, waits for them, and re-layouts  3.26 us (6%)
    pallas_call x1, Pallas kernels, gathered_spectra(): pl.pallas_call(gather_kernel, out_shape=(jax.ShapeDtypeStruct((BLK * LANE...  48.7 us
    unnamed x8, local copies, waits for them, and re-layouts  3.26 us
    pallas_call x1, Pallas kernels, to_time(): pl.pallas_call(functools.partial(to_time_kernel, scale), out_shape=jax.Sh...  3.13 us

profile of v4, /device:TPU:5, one launch (start us, length us, event | category | flops | bytes accessed | tf_op | source)
XLA Modules:
  0.0 55.1 jit_solution(1674025113121041353)
XLA Ops:
  0.0 0.0 copy-start
  0.0 1.2 %copy-done = bf16[2,32,32,256]{3,2,1,0:T(8,128)(2,1)S(1)} copy-done((bf16[2,32,32,256]{3,2,1,0:T(8,128)(2,1)S(1)}, bf16[2,32,32,256]{3,2,1,0:T(8,128)(2,1)}, u32[]{:S(2)}) %copy-start) | copy-done | bytes 1048600
  1.2 0.0 copy-start.1
  1.2 0.7 %copy-done.1 = s32[2,32]{1,0:T(2,128)S(1)} copy-done((s32[2,32]{1,0:T(2,128)S(1)}, s32[2,32]{1,0:T(2,128)}, u32[]{:S(2)}) %copy-start.1) | copy-done | bytes 280
  1.9 0.0 copy-start.2
  1.9 0.7 %copy-done.2 = f32[2,32]{1,0:T(2,128)S(1)} copy-done((f32[2,32]{1,0:T(2,128)S(1)}, f32[2,32]{1,0:T(2,128)}, u32[]{:S(2)}) %copy-start.2) | copy-done | bytes 280
  2.6 0.0 copy-start.3
  2.6 0.7 %copy-done.3 = s32[256]{0:T(256)S(1)} copy-done((s32[256]{0:T(256)S(1)}, s32[256]{0:T(256)}, u32[]{:S(2)}) %copy-start.3) | copy-done | bytes 1048
  3.3 48.7 %gathered_spectra.1 = (f32[4096,128]{1,0:T(8,128)S(1)}, bf16[512,1024]{1,0:T(8,128)(2,1)S(1)}) custom-call(bf16[2,32,32,256]{3,2,1,0:T(8,128)(2,1)S(1)} %copy-done, s32[2,32]{1,0:T(2,128)S(1)} %copy-done.1, f32[2,32]{1,0:T(2,128)S(1)} %copy-done.2, s32[1,256]{1,0:T(1,128)S(1)} %bitcast.1), custom_call_target="tpu_custom_call" | custom-call | flops 268435456 | bytes 4194304 | tf_op jit(solution)/shard_map/gathered_spectra/pallas_call | solution.py:459
  52.0 3.1 %to_time.1 = bf16[32,32,1024]{2,1,0:T(8,128)(2,1)} custom-call(f32[4096,128]{1,0:T(8,128)S(1)} %get-tuple-element.7.z_ref, bf16[512,1024]{1,0:T(8,128)(2,1)S(1)} %get-tuple-element.8.table), custom_call_target="tpu_custom_call" | custom-call | flops 1073741824 | bytes 5242880 | tf_op jit(solution)/shard_map/to_time/pallas_call | solution.py:515
Async XLA Ops:
  0.0 1.2 %copy-start = (bf16[2,32,32,256]{3,2,1,0:T(8,128)(2,1)S(1)}, bf16[2,32,32,256]{3,2,1,0:T(8,128)(2,1)}, u32[]{:S(2)}) copy-start(bf16[2,32,32,256]{3,2,1,0:T(8,128)(2,1)} %data.1) | copy-start | bytes 3145732
  1.2 0.7 %copy-start.1 = (s32[2,32]{1,0:T(2,128)S(1)}, s32[2,32]{1,0:T(2,128)}, u32[]{:S(2)}) copy-start(s32[2,32]{1,0:T(2,128)} %panel_index.1) | copy-start | bytes 772
  1.9 0.7 %copy-start.2 = (f32[2,32]{1,0:T(2,128)S(1)}, f32[2,32]{1,0:T(2,128)}, u32[]{:S(2)}) copy-start(f32[2,32]{1,0:T(2,128)} %panel_weight.1) | copy-start | bytes 772
  2.6 0.7 %copy-start.3 = (s32[256]{0:T(256)S(1)}, s32[256]{0:T(256)}, u32[]{:S(2)}) copy-start(s32[256]{0:T(256)} %param.7) | copy-start | bytes 3076

commit v5 on v4

--- a/solution.py
+++ b/solution.py
@@ -18,7 +18,7 @@
 CH = 2
 NU = 4
 PER = HALF // NU
-ROWS_AT_ONCE = 8
+ROWS_AT_ONCE = 16
 PARTS = 4
 MESH = pl.DeviceIdType.MESH
 
@@ -82,11 +82,11 @@
         arrive(beside)
 
     def turn(block_rows, store):
-        @pl.loop(0, BLK, unroll=2)
+        @pl.loop(0, BLK, unroll=8)
         def _(s):
             turned[pl.ds(s, LANES, stride=BLK), :] = block_rows(s).T
 
-        @pl.loop(0, 2 * HALF, unroll=4)
+        @pl.loop(0, 2 * HALF, unroll=16)
         def _(f):
             store(f, turned[pl.ds(f * BLK, BLK), :].astype(jnp.bfloat16))
 
@@ -371,22 +371,22 @@
     begin_left(3)
     pass_left_on(1, 1)
     begin_right(3)
+    pass_left_on(0, 2)
     pass_left_on(2, 1)
-    pass_left_on(0, 2)
     pass_right_on(0)
+    pass_left_on(1, 2)
     pass_left_on(3, 1)
-    pass_left_on(1, 2)
+    pass_left_on(0, 3)
     pass_right_on(1)
     pass_left_on(2, 2)
-    pass_left_on(0, 3)
+    pass_left_on(1, 3)
+    multiply(0)
     pass_left_on(3, 2)
-    pass_left_on(1, 3)
     pass_right_on(2)
     pass_left_on(2, 3)
-    multiply(0)
+    multiply(1)
     pass_right_on(3)
     pass_left_on(3, 3)
-    multiply(1)
     multiply(2)
     multiply(3)
     for u in range(NU):

time: 55.9 us -> 54.4 us (0.973)
  the two profiles are of different devices: /device:TPU:5 before, /device:TPU:78 now
where the time goes in v5:
time: 54.4 us; the launch traced here: 54.2 us
  Pallas kernels  51 us (94%)
  local copies, waits for them, and re-layouts  3.26 us (6%)
    pallas_call x1, Pallas kernels, gathered_spectra(): pl.pallas_call(gather_kernel, out_shape=(jax.ShapeDtypeStruct((BLK * LANE...  48.4 us
    unnamed x8, local copies, waits for them, and re-layouts  3.26 us
    pallas_call x1, Pallas kernels, to_time(): pl.pallas_call(functools.partial(to_time_kernel, scale), out_shape=jax.Sh...  2.57 us

profile of v5, /device:TPU:78, one launch (start us, length us, event | category | flops | bytes accessed | tf_op | source)
XLA Modules:
  0.0 54.2 jit_solution(12615699173408252980)
XLA Ops:
  0.0 0.0 copy-start
  0.0 1.2 %copy-done = bf16[2,32,32,256]{3,2,1,0:T(8,128)(2,1)S(1)} copy-done((bf16[2,32,32,256]{3,2,1,0:T(8,128)(2,1)S(1)}, bf16[2,32,32,256]{3,2,1,0:T(8,128)(2,1)}, u32[]{:S(2)}) %copy-start) | copy-done | bytes 1048600
  1.2 0.0 copy-start.1
  1.2 0.7 %copy-done.1 = s32[2,32]{1,0:T(2,128)S(1)} copy-done((s32[2,32]{1,0:T(2,128)S(1)}, s32[2,32]{1,0:T(2,128)}, u32[]{:S(2)}) %copy-start.1) | copy-done | bytes 280
  1.9 0.0 copy-start.2
  1.9 0.7 %copy-done.2 = f32[2,32]{1,0:T(2,128)S(1)} copy-done((f32[2,32]{1,0:T(2,128)S(1)}, f32[2,32]{1,0:T(2,128)}, u32[]{:S(2)}) %copy-start.2) | copy-done | bytes 280
  2.6 0.0 copy-start.3
  2.6 0.7 %copy-done.3 = s32[256]{0:T(256)S(1)} copy-done((s32[256]{0:T(256)S(1)}, s32[256]{0:T(256)}, u32[]{:S(2)}) %copy-start.3) | copy-done | bytes 1048
  3.3 48.4 %gathered_spectra.1 = (f32[4096,128]{1,0:T(8,128)S(1)}, bf16[512,1024]{1,0:T(8,128)(2,1)S(1)}) custom-call(bf16[2,32,32,256]{3,2,1,0:T(8,128)(2,1)S(1)} %copy-done, s32[2,32]{1,0:T(2,128)S(1)} %copy-done.1, f32[2,32]{1,0:T(2,128)S(1)} %copy-done.2, s32[1,256]{1,0:T(1,128)S(1)} %bitcast.1), custom_call_target="tpu_custom_call" | custom-call | flops 268435456 | bytes 4194304 | tf_op jit(solution)/shard_map/gathered_spectra/pallas_call | solution.py:459
  51.7 2.6 %to_time.1 = bf16[32,32,1024]{2,1,0:T(8,128)(2,1)} custom-call(f32[4096,128]{1,0:T(8,128)S(1)} %get-tuple-element.7.z_ref, bf16[512,1024]{1,0:T(8,128)(2,1)S(1)} %get-tuple-element.8.table), custom_call_target="tpu_custom_call" | custom-call | flops 1073741824 | bytes 5242880 | tf_op jit(solution)/shard_map/to_time/pallas_call | solution.py:515
Async XLA Ops:
  0.0 1.2 %copy-start = (bf16[2,32,32,256]{3,2,1,0:T(8,128)(2,1)S(1)}, bf16[2,32,32,256]{3,2,1,0:T(8,128)(2,1)}, u32[]{:S(2)}) copy-start(bf16[2,32,32,256]{3,2,1,0:T(8,128)(2,1)} %data.1) | copy-start | bytes 3145732
  1.2 0.7 %copy-start.1 = (s32[2,32]{1,0:T(2,128)S(1)}, s32[2,32]{1,0:T(2,128)}, u32[]{:S(2)}) copy-start(s32[2,32]{1,0:T(2,128)} %panel_index.1) | copy-start | bytes 772
  1.9 0.7 %copy-start.2 = (f32[2,32]{1,0:T(2,128)S(1)}, f32[2,32]{1,0:T(2,128)}, u32[]{:S(2)}) copy-start(f32[2,32]{1,0:T(2,128)} %panel_weight.1) | copy-start | bytes 772
  2.6 0.7 %copy-start.3 = (s32[256]{0:T(256)S(1)}, s32[256]{0:T(256)}, u32[]{:S(2)}) copy-start(s32[256]{0:T(256)} %param.7) | copy-start | bytes 3076
